TPU v7x, 128 devices: a whole 4x4x4 slice. The times are simulated.
128 devices in a mesh: item: 32 (over z, x, core), req: 4 (over y).
Axes of the slice: x: 4, y: 4, z: 4, core: 2. Of those that a mesh axis runs over, the one named last changes fastest.
Arguments:
- user_emb: bfloat16 [128, 256], P('req'), may hold values from -6 to 6
- codebooks: bfloat16 [32, 256, 8], P('item'), may hold values from -1 to 1
- item_codes: int32 [131072, 32], P('item'), may hold values from 0 to 255
- item_place: int32 [131072], replicated, may hold values from 0 to 131071, as said below
- candidates: int32 [128, 512], P('req', 'item'), may hold values from 0 to 131071, as said below
- item_features: bfloat16 [131072, 768], P(('item', 'req')), may hold values from -6 to 6
- cross_weights: bfloat16 [4, 1024, 1024], replicated, may hold values from -0.25 to 0.25
- cross_bias: float32 [4, 1024], replicated, may hold values from -6 to 6
- out_weight: float32 [1024], replicated, may hold values from -0.5 to 0.5
Outputs:
- scores: float32 [128, 131072], P('req', 'item')
- logits: float32 [128, 512], P('req', 'item')
Inputs may be any that keep to these rules, and one draw needn't show every extreme that they name: A permutation of the item ids: item_place[i] is the storage row of item i; storage row s is held by the device at flat index s // 1024 of item+req (item slowest). Item ids. In each aligned block of 32 requests by 16 candidates (one device's share), at most 12 candidates have storage rows on any one owner; in every draw one owner, the same for all blocks, is named exactly 12 times in every block.
All inputs are finite; a program needn't handle non-finite values.
Results may differ from a plain program's by a relative error of at most 0.0033.
Values may be sent and summed in bfloat16 or wider, within the bound.
No kernel may reach another device: no remote copies, remote signals or barrier semaphores. Data moves between devices by JAX's collectives and lax.ppermute only.
A program may use at most 64 MiB of HBM per device.

v0:
```python
import jax
import jax.numpy as jnp
from jax import lax
from jax.sharding import PartitionSpec as P

M = 32


def score_tables(total, tables, item_codes):
    width_all = tables.shape[1]
    codes_count = tables.shape[2]
    code_range = lax.iota(jnp.int32, codes_count)[None, None, :]
    for group in range(0, width_all, 4):
        width = min(4, width_all - group)
        codes_now = lax.dynamic_slice_in_dim(item_codes, group, width, 1)
        onehot = (codes_now[:, :, None] == code_range).astype(jnp.bfloat16)
        total = total + jnp.einsum(
            "rmk,imk->ri",
            tables[:, group : group + width],
            onehot,
            preferred_element_type=jnp.float32,
        )
    return total


def on_device(
    user_emb,
    codebooks,
    item_codes,
    item_place,
    candidates,
    item_features,
    cross_weights,
    cross_bias,
    out_weight,
):
    requests = user_emb.shape[0]
    local_sub = codebooks.shape[0]
    sub_width = codebooks.shape[2]
    parts = user_emb.reshape(requests, M, sub_width)
    empty = jnp.zeros((requests, item_codes.shape[0]), jnp.float32)
    first_sub = lax.axis_index("item") * local_sub
    mine = lax.dynamic_slice_in_dim(parts, first_sub, local_sub, 1)
    tables = jnp.einsum("rms,mks->rmk", mine, codebooks, preferred_element_type=jnp.float32).astype(
        jnp.bfloat16
    )
    scores = score_tables(empty, lax.all_gather(tables, "item", axis=1, tiled=True), item_codes)
    cand_dev = candidates.shape[1]
    rows_dev = item_features.shape[0]
    item_count = lax.axis_size("item")
    req_count = lax.axis_size("req")
    owners = item_count * req_count
    total_rows = requests * cand_dev
    capacity = 3 * total_rows // owners
    slots = jnp.take(item_place, candidates.reshape(-1), axis=0)
    owner = slots // rows_dev
    within = slots % rows_dev
    owner_hits = (owner[:, None] == jnp.arange(owners, dtype=jnp.int32)[None, :]).astype(jnp.int32)
    ranks = jnp.sum((jnp.cumsum(owner_hits, axis=0) - owner_hits) * owner_hits, axis=1)
    wanted = jnp.zeros((owners, capacity), jnp.int32).at[owner, ranks].set(within)
    found = jnp.take(
        item_features,
        lax.all_to_all(wanted, ("item", "req"), split_axis=0, concat_axis=0, tiled=True),
        axis=0,
    )
    fetched = lax.all_to_all(found, ("item", "req"), split_axis=0, concat_axis=0, tiled=True)
    item_rows = fetched[owner, ranks]
    repeated = jnp.repeat(user_emb, cand_dev, axis=0)
    first = jnp.concatenate([repeated, item_rows], axis=1)
    state = first.astype(jnp.float32)
    for layer in range(cross_weights.shape[0]):
        product = (
            jnp.dot(
                state.astype(jnp.bfloat16), cross_weights[layer], preferred_element_type=jnp.float32
            )
            + cross_bias[layer]
        )
        state = first * product + state
    logits = jnp.sum(state * out_weight, axis=1).reshape(requests, cand_dev)
    return (scores, logits)


def solution(mesh):
    placed = (
        P("req", None),
        P("item", None, None),
        P("item", None),
        P(),
        P("req", "item"),
        P(("item", "req"), None),
        P(),
        P(),
        P(),
    )
    return jax.shard_map(
        on_device,
        mesh=mesh,
        in_specs=placed,
        out_specs=(P("req", "item"), P("req", "item")),
        check_vma=False,
    )
```

profile of v0, /device:TPU:1, one launch (start us, length us, event | category | flops | bytes accessed | tf_op | source)
XLA Modules:
  0.0 162.4 jit_solution(7211599996360040882)
XLA Ops:
  0.6 0.9 copy.22
  1.8 6.5 %gather_fusion = s32[512]{0:T(512)S(1)} fusion(s32[131072]{0:T(1024)} %param.12, s32[1024]{0:T(1024)S(1)} %pad_clamp_fusion.1), kind=kCustom, calls=%fused_computation | custom fusion | bytes 6144 | tf_op jit(solution)/shard_map/jit(_take)/gather | solution.py:55
  8.3 0.1 copy.25
  8.5 0.2 fusion.62
  8.8 0.2 fusion.61
  9.1 24.6 %scatter_fusion = s32[128,12]{0,1:T(8,128)S(1)} fusion(s32[128,12]{0,1:T(8,128)S(1)} %broadcast_in_dim.27, s32[512]{0:T(512)S(1)} %bitcast.106, s32[512]{0:T(512)S(1)} %get-tuple-element.20), kind=kCustom, calls=%fused_computation.3 | custom fusion | bytes 10240 | tf_op jit(solution)/shard_map/scatter | solution.py:60
  33.7 0.7 copy.27
  34.5 11.5 %all-to-all-start = ((s32[128,1,12]{2,1,0:T(1,128)}), s32[128,1,12]{2,1,0:T(1,128)S(1)}, u32[]{:S(2)}, u32[]{:S(2)}) async-start(s32[128,1,12]{2,1,0:T(1,128)} %copy.27), calls=%async_computation | async-start | bytes 131072 | tf_op jit(solution)/shard_map/all_to_all | solution.py:63
  46.0 0.1 copy.21
  46.2 0.2 fusion.55
  46.4 25.8 %all_gather.3 = bf16[32,32,256]{2,0,1:T(8,128)(2,1)S(1)} all-gather(bf16[32,1,256]{2,0,1:T(8,128)(2,1)S(1)} %fusion.55), channel_id=1, replica_groups=mesh['item'=32,'req'=4] {'item'}, dimensions={1}, use_global_device_ids=true | all-gather | bytes 540672 | tf_op jit(solution)/shard_map/all_gather | solution.py:47
  72.2 0.1 reshape.248
  72.3 5.7 %gather_fusion.1 = bf16[1536,768]{1,0:T(8,128)(2,1)} fusion(bf16[1024,768]{1,0:T(8,128)(2,1)S(1)} %copy-done, s32[2048]{0:T(1024)S(1)} %pad_clamp_fusion), kind=kCustom, calls=%fused_computation.1 | custom fusion | bytes 4724736 | tf_op jit(solution)/shard_map/jit(_take)/gather | solution.py:61
  78.0 4.9 %reshape.247 = bf16[128,12,768]{2,1,0:T(8,128)(2,1)} reshape(bf16[1536,768]{1,0:T(8,128)(2,1)} %gather_fusion.1) | data formatting | bytes 4718592 | tf_op jit(solution)/shard_map/jit(_take)/gather | solution.py:61
  83.0 0.1 copy.29
  83.1 3.3 %broadcast_select_fusion = bf16[128,12,768]{2,1,0:T(8,128)(2,1)} fusion(bf16[128,12,768]{2,1,0:T(8,128)(2,1)} %reshape.247, pred[128,12]{1,0:T(8,128)(4,1)S(1)} %copy.29), kind=kLoop, calls=%fused_computation.48 | loop fusion | flops 1179648 | bytes 4720128 | tf_op jit(solution)/shard_map/jit(_take)/select_n | solution.py:61
  86.4 7.5 %all-to-all-start.1 = ((bf16[128,12,768]{2,1,0:T(8,128)(2,1)}), bf16[128,12,768]{2,1,0:T(8,128)(2,1)}, u32[]{:S(2)}, u32[]{:S(2)}) async-start(bf16[128,12,768]{2,1,0:T(8,128)(2,1)} %broadcast_select_fusion), calls=%async_computation.1 | async-start | bytes 6291456 | tf_op jit(solution)/shard_map/all_to_all | solution.py:66
  94.0 5.9 %fusion.16 = f32[32,4096]{1,0:T(8,128)S(1)} fusion(bf16[32,32,256]{2,0,1:T(8,128)(2,1)S(1)} %all_gather.3, s32[4096,4]{0,1:T(4,128)S(1)} %get-tuple-element.14), kind=kOutput, calls=%fused_computation.28 | convolution fusion | flops 272629760 | bytes 1114112 | tf_op jit(solution)/shard_map/rmk,imk->ri/dot_general | solution.py:17
  99.9 5.9 %fusion.17 = f32[32,4096]{1,0:T(8,128)S(1)} fusion(bf16[32,32,256]{2,0,1:T(8,128)(2,1)S(1)} %all_gather.3, s32[4096,4]{0,1:T(4,128)S(1)} %get-tuple-element.15), kind=kOutput, calls=%fused_computation.29 | convolution fusion | flops 272629760 | bytes 1114112 | tf_op jit(solution)/shard_map/rmk,imk->ri/dot_general | solution.py:17
  105.8 5.9 %fusion.18 = f32[32,4096]{1,0:T(8,128)S(1)} fusion(bf16[32,32,256]{2,0,1:T(8,128)(2,1)S(1)} %all_gather.3, s32[4096,4]{0,1:T(4,128)S(1)} %get-tuple-element.9), kind=kOutput, calls=%fused_computation.30 | convolution fusion | flops 272629760 | bytes 1114112 | tf_op jit(solution)/shard_map/rmk,imk->ri/dot_general | solution.py:17
  111.8 5.9 %fusion.19 = f32[32,4096]{1,0:T(8,128)S(1)} fusion(bf16[32,32,256]{2,0,1:T(8,128)(2,1)S(1)} %all_gather.3, s32[4096,4]{0,1:T(4,128)S(1)} %get-tuple-element.10), kind=kOutput, calls=%fused_computation.31 | convolution fusion | flops 272629760 | bytes 1114112 | tf_op jit(solution)/shard_map/rmk,imk->ri/dot_general | solution.py:17
  117.7 5.9 %fusion.20 = f32[32,4096]{1,0:T(8,128)S(1)} fusion(bf16[32,32,256]{2,0,1:T(8,128)(2,1)S(1)} %all_gather.3, s32[4096,4]{0,1:T(4,128)S(1)} %get-tuple-element.11), kind=kOutput, calls=%fused_computation.32 | convolution fusion | flops 272629760 | bytes 1114112 | tf_op jit(solution)/shard_map/rmk,imk->ri/dot_general | solution.py:17
  123.7 5.9 %fusion.21 = f32[32,4096]{1,0:T(8,128)S(1)} fusion(bf16[32,32,256]{2,0,1:T(8,128)(2,1)S(1)} %all_gather.3, s32[4096,4]{0,1:T(4,128)S(1)} %get-tuple-element.12), kind=kOutput, calls=%fused_computation.33 | convolution fusion | flops 272629760 | bytes 1114112 | tf_op jit(solution)/shard_map/rmk,imk->ri/dot_general | solution.py:17
  129.6 5.9 %fusion.22 = f32[32,4096]{1,0:T(8,128)S(1)} fusion(bf16[32,32,256]{2,0,1:T(8,128)(2,1)S(1)} %all_gather.3, s32[4096,4]{0,1:T(4,128)S(1)} %get-tuple-element.13), kind=kOutput, calls=%fused_computation.34 | convolution fusion | flops 272629760 | bytes 1114112 | tf_op jit(solution)/shard_map/rmk,imk->ri/dot_general | solution.py:17
  135.6 5.5 %fusion.30 = f32[32,4096]{1,0:T(8,128)} fusion(f32[32,4096]{1,0:T(8,128)S(1)} %fusion.16, f32[32,4096]{1,0:T(8,128)S(1)} %fusion.17, f32[32,4096]{1,0:T(8,128)S(1)} %fusion.18, f32[32,4096]{1,0:T(8,128)S(1)} %fusion.19, f32[32,4096]{1,0:T(8,128)S(1)} %fusion.20, f32[32,4096]{1,0:T(8,128)S(1)} %fusion.21, f32[32,4096]{1,0:T(8,128)S(1)} %fusion.22, ...), kind=kOutput, calls=%fused_computation.42 | convolution fusion | flops 273547264 | bytes 4784128 | tf_op jit(solution)/shard_map/rmk,imk->ri/dot_general | solution.py:17
  141.0 4.1 %copy.30 = bf16[128,12,768]{2,0,1:T(8,128)(2,1)} copy(bf16[128,12,768]{2,1,0:T(8,128)(2,1)} %all-to-all-done.1) | data formatting | bytes 4718592 | tf_op jit(solution)/shard_map/all_to_all | solution.py:66
  145.1 7.3 %gather_fusion.2 = bf16[512,768]{1,0:T(8,128)(2,1)S(1)} fusion(bf16[128,12,768]{2,0,1:T(8,128)(2,1)} %copy.30, s32[512]{0:T(512)S(1)} %bitcast.105), kind=kCustom, calls=%fused_computation.2 | custom fusion | bytes 1576960 | tf_op jit(solution)/shard_map/gather | solution.py:67
  152.4 3.0 %fusion.42 = f32[512,1024]{1,0:T(8,128)S(1)} fusion(bf16[4,1024,1024]{2,1,0:T(8,128)(2,1)} %param.15, bf16[512,768]{1,0:T(8,128)(2,1)S(1)} %gather_fusion.2, bf16[512,256]{1,0:T(8,128)(2,1)S(1)} %bitcast.110), kind=kOutput, calls=%fused_computation.60 | convolution fusion | flops 1075838976 | bytes 5242880 | tf_op jit(solution)/shard_map/dot_general | solution.py:73
  155.5 3.2 %fusion.31 = f32[512,1024]{1,0:T(8,128)S(1)} fusion(f32[512,1024]{1,0:T(8,128)S(1)} %fusion.42, bf16[4,1024,1024]{2,1,0:T(8,128)(2,1)} %param.15, f32[1024]{0:T(1024)S(1)} %bitcast.121, f32[1024]{0:T(1024)S(1)} %bitcast.122, bf16[512,768]{1,0:T(8,128)(2,1)S(1)} %gather_fusion.2, bf16[512,256]{1,0:T(8,128)(2,1)S(1)} %bitcast.111), kind=kOutput, calls=%fused_computation.49 | convolution fusion | flops 1083179008 | bytes 10498048 | tf_op jit(solution)/shard_map/dot_general | solution.py:73
  158.8 1.3 fusion.32
  160.1 1.5 fusion.35
  161.8 0.7 copy.31
  (42 shorter events, 0.8 us)
Async XLA Ops:
  0.6 71.7 %copy-start = (bf16[1024,768]{1,0:T(8,128)(2,1)S(1)}, bf16[1024,768]{1,0:T(8,128)(2,1)}, u32[]{:S(2)}) copy-start(bf16[1024,768]{1,0:T(8,128)(2,1)} %param.14) | copy-start | bytes 4718596
  9.1 36.9 %copy-start.2 = (bf16[32,256]{1,0:T(8,128)(2,1)S(1)}, bf16[32,256]{1,0:T(8,128)(2,1)}, u32[]{:S(2)}) copy-start(bf16[32,256]{1,0:T(8,128)(2,1)} %param.9) | copy-start | bytes 49156
  9.1 37.0 %copy-start.1 = (s32[4096,32]{0,1:T(8,128)S(1)}, s32[4096,32]{0,1:T(8,128)}, u32[]{:S(2)}) copy-start(s32[4096,32]{0,1:T(8,128)} %param.11) | copy-start | bytes 1572868
  9.1 37.1 %copy-start.4 = (bf16[1,256,8]{1,2,0:T(8,128)(2,1)S(1)}, bf16[1,256,8]{1,2,0:T(8,128)(2,1)}, u32[]{:S(2)}) copy-start(bf16[1,256,8]{1,2,0:T(8,128)(2,1)} %param.10) | copy-start | bytes 12292
  34.5 37.7 %all-to-all-start = ((s32[128,1,12]{2,1,0:T(1,128)}), s32[128,1,12]{2,1,0:T(1,128)S(1)}, u32[]{:S(2)}, u32[]{:S(2)}) async-start(s32[128,1,12]{2,1,0:T(1,128)} %copy.27), calls=%async_computation | async-start | bytes 131072 | tf_op jit(solution)/shard_map/all_to_all | solution.py:63
  86.4 7.5 %copy-start.3 = (f32[4,1024]{1,0:T(4,128)S(1)}, f32[4,1024]{1,0:T(4,128)}, u32[]{:S(2)}) copy-start(f32[4,1024]{1,0:T(4,128)} %param.16) | copy-start | bytes 49156
  86.4 54.6 %all-to-all-start.1 = ((bf16[128,12,768]{2,1,0:T(8,128)(2,1)}), bf16[128,12,768]{2,1,0:T(8,128)(2,1)}, u32[]{:S(2)}, u32[]{:S(2)}) async-start(bf16[128,12,768]{2,1,0:T(8,128)(2,1)} %broadcast_select_fusion), calls=%async_computation.1 | async-start | bytes 6291456 | tf_op jit(solution)/shard_map/all_to_all | solution.py:66
  152.4 6.3 %slice-start = ((s8[8388608]{0:T(1024)(128)(4,1)}), s8[4194304]{0:T(1024)(128)(4,1)S(1)}, s32[]{:S(2)}) async-start(s8[8388608]{0:T(1024)(128)(4,1)} %bitcast.123), calls=%async_computation.2 | async-start | bytes 8388608
  155.5 3.3 %slice-start.1 = ((s8[8388608]{0:T(1024)(128)(4,1)}), s8[4194304]{0:T(1024)(128)(4,1)S(1)}, s32[]{:S(2)}) async-start(s8[8388608]{0:T(1024)(128)(4,1)} %bitcast.123), calls=%async_computation.3 | async-start | bytes 8388608
  158.8 1.4 copy-start.5
where the time goes:
time: 163 us; the launch traced here: 162 us
  local copies, waits for them, and re-layouts  56.4 us (35%)
  matrix products  56.4 us (35%)
  blocking collectives  25.8 us (16%)
  starting transfers between devices  19 us (12%)
  other arithmetic  3.91 us (2%)
    dot_general x8, matrix products, score_tables(): jnp.einsum('rmk,imk->ri', tables[:, group:group + width], onehot, preferr...  47 us
    all_gather x1, blocking collectives, on_device(): lax.all_gather(tables, 'item', axis=1, tiled=True)  25.8 us
    scatter x1, local copies, waits for them, and re-layouts, on_device(): jnp.zeros((owners, capacity), jnp.int32).at[owner, ranks].set(within)  24.6 us
    all_to_all x1, starting transfers between devices, on_device(): lax.all_to_all(wanted, ('item', 'req'), split_axis=0, concat_axis=0, tile...  11.5 us
    gather x2, local copies, waits for them, and re-layouts, on_device(): jnp.take(item_features, lax.all_to_all(wanted, ('item', 'req'), split_axi...  10.5 us
    dot_general x4, matrix products, on_device(): jnp.dot(state.astype(jnp.bfloat16), cross_weights[layer], preferred_eleme...  9.15 us
    all_to_all x1, starting transfers between devices, on_device(): lax.all_to_all(found, ('item', 'req'), split_axis=0, concat_axis=0, tiled...  7.49 us
    gather x1, local copies, waits for them, and re-layouts, on_device(): item_rows = fetched[owner, ranks]  7.29 us
  transfers between devices with their start and end apart: 2, of which 0 were waited for; matrix products, arithmetic and copies ran while one was open for 29% of the time, Pallas kernels for 0%

commit v1 on v0

--- a/solution.py
+++ b/solution.py
@@ -44,7 +44,13 @@
     tables = jnp.einsum("rms,mks->rmk", mine, codebooks, preferred_element_type=jnp.float32).astype(
         jnp.bfloat16
     )
-    scores = score_tables(empty, lax.all_gather(tables, "item", axis=1, tiled=True), item_codes)
+    scores = score_tables(
+        empty,
+        jnp.concatenate(
+            lax.all_to_all(jnp.stack([tables] * lax.axis_size("item")), "item", 0, 0), axis=1
+        ),
+        item_codes,
+    )
     cand_dev = candidates.shape[1]
     rows_dev = item_features.shape[0]
     item_count = lax.axis_size("item")

time: 163 us -> 152 us (0.933)
  blocking collectives: 25.8 us -> 0 us
  waiting for transfers between devices: 0.01 us -> 9.13 us
  starting transfers between devices: 19 us -> 23.9 us
    all_gather x1 -> x0, blocking collectives: 25.8 us -> none  [on_device(): lax.all_gather(tables, 'item', axis=1, tiled=True)]
    all_to_all x1, waiting for transfers between devices: 0.01 us -> 9.12 us  [on_device(): lax.all_to_all(wanted, ('item', 'req'), split_axis=0, concat_axis=0, tile...]
    all_to_all x0 -> x1, starting transfers between devices: none -> 4.28 us  [on_device(): lax.all_to_all(jnp.stack([tables] * lax.axis_size('item')), 'item', 0, 0)]
  transfers between devices with their start and end apart: 2 -> 3, of which waited for: 0 -> 1; matrix products, arithmetic and copies ran while one was open for 29% -> 41% of each run, Pallas kernels for 0% -> 0%
where the time goes in v1:
time: 152 us
  local copies, waits for them, and re-layouts  57.2 us (38%)
  matrix products  56.4 us (37%)
  starting transfers between devices  23.9 us (16%)
  waiting for transfers between devices  9.13 us (6%)
  other arithmetic  3.92 us (3%)
    dot_general x8, matrix products, score_tables(): jnp.einsum('rmk,imk->ri', tables[:, group:group + width], onehot, preferr...  47 us
    scatter x1, local copies, waits for them, and re-layouts, on_device(): jnp.zeros((owners, capacity), jnp.int32).at[owner, ranks].set(within)  24.6 us
    all_to_all x1, starting transfers between devices, on_device(): lax.all_to_all(wanted, ('item', 'req'), split_axis=0, concat_axis=0, tile...  11.5 us
    gather x2, local copies, waits for them, and re-layouts, on_device(): jnp.take(item_features, lax.all_to_all(wanted, ('item', 'req'), split_axi...  10.5 us
    dot_general x4, matrix products, on_device(): jnp.dot(state.astype(jnp.bfloat16), cross_weights[layer], preferred_eleme...  9.14 us
    all_to_all x1, waiting for transfers between devices, on_device(): lax.all_to_all(wanted, ('item', 'req'), split_axis=0, concat_axis=0, tile...  9.12 us
    all_to_all x1, starting transfers between devices, on_device(): lax.all_to_all(found, ('item', 'req'), split_axis=0, concat_axis=0, tiled...  8.09 us
    gather x1, local copies, waits for them, and re-layouts, on_device(): item_rows = fetched[owner, ranks]  7.3 us
  transfers between devices with their start and end apart: 3, of which 1 were waited for; matrix products, arithmetic and copies ran while one was open for 41% of the time, Pallas kernels for 0%

profile of v1, /device:TPU:1, one launch (start us, length us, event | category | flops | bytes accessed | tf_op | source)
XLA Modules:
  0.0 151.5 jit_solution(1640663232162696519)
XLA Ops:
  0.6 0.9 copy.23
  1.8 6.5 %gather_fusion = s32[512]{0:T(512)S(1)} fusion(s32[131072]{0:T(1024)} %param.12, s32[1024]{0:T(1024)S(1)} %pad_clamp_fusion.1), kind=kCustom, calls=%fused_computation | custom fusion | bytes 6144 | tf_op jit(solution)/shard_map/jit(_take)/gather | solution.py:61
  8.5 0.2 fusion.69
  8.8 0.2 fusion.68
  9.1 24.6 %scatter_fusion = s32[128,12]{0,1:T(8,128)S(1)} fusion(s32[128,12]{0,1:T(8,128)S(1)} %broadcast_in_dim.27, s32[512]{0:T(512)S(1)} %bitcast.113, s32[512]{0:T(512)S(1)} %get-tuple-element.20), kind=kCustom, calls=%fused_computation.3 | custom fusion | bytes 10240 | tf_op jit(solution)/shard_map/scatter | solution.py:66
  33.7 0.7 copy.28
  34.5 11.5 %all-to-all-start.1 = ((s32[128,1,12]{2,1,0:T(1,128)}), s32[128,1,12]{2,1,0:T(1,128)S(1)}, u32[]{:S(2)}, u32[]{:S(2)}) async-start(s32[128,1,12]{2,1,0:T(1,128)} %copy.28), calls=%async_computation.1 | async-start | bytes 131072 | tf_op jit(solution)/shard_map/all_to_all | solution.py:69
  46.0 0.1 copy.21
  46.2 0.2 convolution_convert_fusion
  46.4 9.1 %all-to-all-done.1 = s32[128,1,12]{2,1,0:T(1,128)S(1)} async-done(((s32[128,1,12]{2,1,0:T(1,128)}), s32[128,1,12]{2,1,0:T(1,128)S(1)}, u32[]{:S(2)}, u32[]{:S(2)}) %all-to-all-start.1) | async-done | bytes 6176 | tf_op jit(solution)/shard_map/all_to_all | solution.py:69
  55.5 0.9 stack.2
  56.4 4.3 %all-to-all-start = ((bf16[32,32,1,256]{3,1,2,0:T(8,128)(2,1)}), bf16[32,32,1,256]{3,1,2,0:T(8,128)(2,1)S(1)}, u32[]{:S(2)}, u32[]{:S(2)}) async-start(bf16[32,32,1,256]{3,1,2,0:T(8,128)(2,1)} %stack.2), calls=%async_computation | async-start | bytes 1048576 | tf_op jit(solution)/shard_map/all_to_all | solution.py:50
  60.8 5.7 %gather_fusion.1 = bf16[1536,768]{1,0:T(8,128)(2,1)} fusion(bf16[1024,768]{1,0:T(8,128)(2,1)S(1)} %copy-done, s32[2048]{0:T(1024)S(1)} %pad_clamp_fusion), kind=kCustom, calls=%fused_computation.1 | custom fusion | bytes 4724736 | tf_op jit(solution)/shard_map/jit(_take)/gather | solution.py:67
  66.5 4.9 %reshape.258 = bf16[128,12,768]{2,1,0:T(8,128)(2,1)} reshape(bf16[1536,768]{1,0:T(8,128)(2,1)} %gather_fusion.1) | data formatting | bytes 4718592 | tf_op jit(solution)/shard_map/jit(_take)/gather | solution.py:67
  71.4 0.1 copy.30
  71.6 3.3 %broadcast_select_fusion = bf16[128,12,768]{2,1,0:T(8,128)(2,1)} fusion(bf16[128,12,768]{2,1,0:T(8,128)(2,1)} %reshape.258, pred[128,12]{1,0:T(8,128)(4,1)S(1)} %copy.30), kind=kLoop, calls=%fused_computation.48 | loop fusion | flops 1179648 | bytes 4720128 | tf_op jit(solution)/shard_map/jit(_take)/select_n | solution.py:67
  74.9 8.1 %all-to-all-start.2 = ((bf16[128,12,768]{2,1,0:T(8,128)(2,1)}), bf16[128,12,768]{2,1,0:T(8,128)(2,1)}, u32[]{:S(2)}, u32[]{:S(2)}) async-start(bf16[128,12,768]{2,1,0:T(8,128)(2,1)} %broadcast_select_fusion), calls=%async_computation.2 | async-start | bytes 6291456 | tf_op jit(solution)/shard_map/all_to_all | solution.py:72
  83.0 5.9 %fusion.17 = f32[32,4096]{1,0:T(8,128)S(1)} fusion(s32[4096,4]{0,1:T(4,128)S(1)} %get-tuple-element.15, bf16[32,32,1,256]{3,1,2,0:T(8,128)(2,1)S(1)} %all-to-all-done), kind=kOutput, calls=%fused_computation.29 | convolution fusion | flops 272629760 | bytes 1114112 | tf_op jit(solution)/shard_map/rmk,imk->ri/dot_general | solution.py:17
  89.0 5.9 %fusion.18 = f32[32,4096]{1,0:T(8,128)S(1)} fusion(s32[4096,4]{0,1:T(4,128)S(1)} %get-tuple-element.9, bf16[32,32,1,256]{3,1,2,0:T(8,128)(2,1)S(1)} %all-to-all-done), kind=kOutput, calls=%fused_computation.30 | convolution fusion | flops 272629760 | bytes 1114112 | tf_op jit(solution)/shard_map/rmk,imk->ri/dot_general | solution.py:17
  94.9 5.9 %fusion.19 = f32[32,4096]{1,0:T(8,128)S(1)} fusion(s32[4096,4]{0,1:T(4,128)S(1)} %get-tuple-element.10, bf16[32,32,1,256]{3,1,2,0:T(8,128)(2,1)S(1)} %all-to-all-done), kind=kOutput, calls=%fused_computation.31 | convolution fusion | flops 272629760 | bytes 1114112 | tf_op jit(solution)/shard_map/rmk,imk->ri/dot_general | solution.py:17
  100.9 5.9 %fusion.20 = f32[32,4096]{1,0:T(8,128)S(1)} fusion(s32[4096,4]{0,1:T(4,128)S(1)} %get-tuple-element.11, bf16[32,32,1,256]{3,1,2,0:T(8,128)(2,1)S(1)} %all-to-all-done), kind=kOutput, calls=%fused_computation.32 | convolution fusion | flops 272629760 | bytes 1114112 | tf_op jit(solution)/shard_map/rmk,imk->ri/dot_general | solution.py:17
  106.8 5.9 %fusion.21 = f32[32,4096]{1,0:T(8,128)S(1)} fusion(s32[4096,4]{0,1:T(4,128)S(1)} %get-tuple-element.12, bf16[32,32,1,256]{3,1,2,0:T(8,128)(2,1)S(1)} %all-to-all-done), kind=kOutput, calls=%fused_computation.33 | convolution fusion | flops 272629760 | bytes 1114112 | tf_op jit(solution)/shard_map/rmk,imk->ri/dot_general | solution.py:17
  112.8 5.9 %fusion.22 = f32[32,4096]{1,0:T(8,128)S(1)} fusion(s32[4096,4]{0,1:T(4,128)S(1)} %get-tuple-element.13, bf16[32,32,1,256]{3,1,2,0:T(8,128)(2,1)S(1)} %all-to-all-done), kind=kOutput, calls=%fused_computation.34 | convolution fusion | flops 272629760 | bytes 1114112 | tf_op jit(solution)/shard_map/rmk,imk->ri/dot_general | solution.py:17
  118.7 5.9 %fusion.16 = f32[32,4096]{1,0:T(8,128)S(1)} fusion(s32[4096,4]{0,1:T(4,128)S(1)} %get-tuple-element.14, bf16[32,32,1,256]{3,1,2,0:T(8,128)(2,1)S(1)} %all-to-all-done), kind=kOutput, calls=%fused_computation.28 | convolution fusion | flops 272629760 | bytes 1114112 | tf_op jit(solution)/shard_map/rmk,imk->ri/dot_general | solution.py:17
  124.7 5.5 %fusion.30 = f32[32,4096]{1,0:T(8,128)} fusion(f32[32,4096]{1,0:T(8,128)S(1)} %fusion.16, f32[32,4096]{1,0:T(8,128)S(1)} %fusion.17, f32[32,4096]{1,0:T(8,128)S(1)} %fusion.18, f32[32,4096]{1,0:T(8,128)S(1)} %fusion.19, f32[32,4096]{1,0:T(8,128)S(1)} %fusion.20, f32[32,4096]{1,0:T(8,128)S(1)} %fusion.21, f32[32,4096]{1,0:T(8,128)S(1)} %fusion.22, ...), kind=kOutput, calls=%fused_computation.42 | convolution fusion | flops 273547264 | bytes 4784128 | tf_op jit(solution)/shard_map/rmk,imk->ri/dot_general | solution.py:17
  130.1 4.1 %copy.31 = bf16[128,12,768]{2,0,1:T(8,128)(2,1)} copy(bf16[128,12,768]{2,1,0:T(8,128)(2,1)} %all-to-all-done.2) | data formatting | bytes 4718592 | tf_op jit(solution)/shard_map/all_to_all | solution.py:72
  134.2 7.3 %gather_fusion.2 = bf16[512,768]{1,0:T(8,128)(2,1)S(1)} fusion(bf16[128,12,768]{2,0,1:T(8,128)(2,1)} %copy.31, s32[512]{0:T(512)S(1)} %bitcast.112), kind=kCustom, calls=%fused_computation.2 | custom fusion | bytes 1576960 | tf_op jit(solution)/shard_map/gather | solution.py:73
  141.6 3.0 %fusion.42 = f32[512,1024]{1,0:T(8,128)S(1)} fusion(bf16[4,1024,1024]{2,1,0:T(8,128)(2,1)} %param.15, bf16[512,768]{1,0:T(8,128)(2,1)S(1)} %gather_fusion.2, bf16[512,256]{1,0:T(8,128)(2,1)S(1)} %bitcast.117), kind=kOutput, calls=%fused_computation.60 | convolution fusion | flops 1075838976 | bytes 5242880 | tf_op jit(solution)/shard_map/dot_general | solution.py:79
  144.6 3.2 %fusion.31 = f32[512,1024]{1,0:T(8,128)S(1)} fusion(f32[512,1024]{1,0:T(8,128)S(1)} %fusion.42, bf16[4,1024,1024]{2,1,0:T(8,128)(2,1)} %param.15, f32[1024]{0:T(1024)S(1)} %bitcast.128, f32[1024]{0:T(1024)S(1)} %bitcast.129, bf16[512,768]{1,0:T(8,128)(2,1)S(1)} %gather_fusion.2, bf16[512,256]{1,0:T(8,128)(2,1)S(1)} %bitcast.118), kind=kOutput, calls=%fused_computation.49 | convolution fusion | flops 1083179008 | bytes 10498048 | tf_op jit(solution)/shard_map/dot_general | solution.py:79
  147.9 1.3 fusion.32
  149.2 1.5 %fusion.35 = f32[512]{0:T(512)S(1)} fusion(f32[512,1024]{1,0:T(8,128)S(1)} %fusion.32, bf16[4,1024,1024]{2,1,0:T(8,128)(2,1)S(1)} %bitcast.131, f32[1024]{0:T(1024)S(1)} %copy-done.5, f32[1024]{0:T(1024)S(1)} %bitcast.126, bf16[512,768]{1,0:T(8,128)(2,1)S(1)} %gather_fusion.2, bf16[512,256]{1,0:T(8,128)(2,1)S(1)} %bitcast.120), kind=kOutput, calls=%fused_computation.53 | convolution fusion | flops 1078984192 | bytes 7350272 | tf_op jit(solution)/shard_map/dot_general | solution.py:79
  150.9 0.7 copy.32
  (44 shorter events, 1.0 us)
Async XLA Ops:
  0.6 60.2 %copy-start = (bf16[1024,768]{1,0:T(8,128)(2,1)S(1)}, bf16[1024,768]{1,0:T(8,128)(2,1)}, u32[]{:S(2)}) copy-start(bf16[1024,768]{1,0:T(8,128)(2,1)} %param.14) | copy-start | bytes 4718596
  9.1 36.9 %copy-start.2 = (bf16[32,256]{1,0:T(8,128)(2,1)S(1)}, bf16[32,256]{1,0:T(8,128)(2,1)}, u32[]{:S(2)}) copy-start(bf16[32,256]{1,0:T(8,128)(2,1)} %param.9) | copy-start | bytes 49156
  9.1 37.0 %copy-start.1 = (s32[4096,32]{0,1:T(8,128)S(1)}, s32[4096,32]{0,1:T(8,128)}, u32[]{:S(2)}) copy-start(s32[4096,32]{0,1:T(8,128)} %param.11) | copy-start | bytes 1572868
  9.1 37.1 %copy-start.4 = (bf16[1,256,8]{1,2,0:T(8,128)(2,1)S(1)}, bf16[1,256,8]{1,2,0:T(8,128)(2,1)}, u32[]{:S(2)}) copy-start(bf16[1,256,8]{1,2,0:T(8,128)(2,1)} %param.10) | copy-start | bytes 12292
  34.5 21.1 %all-to-all-start.1 = ((s32[128,1,12]{2,1,0:T(1,128)}), s32[128,1,12]{2,1,0:T(1,128)S(1)}, u32[]{:S(2)}, u32[]{:S(2)}) async-start(s32[128,1,12]{2,1,0:T(1,128)} %copy.28), calls=%async_computation.1 | async-start | bytes 131072 | tf_op jit(solution)/shard_map/all_to_all | solution.py:69
  56.4 18.5 %all-to-all-start = ((bf16[32,32,1,256]{3,1,2,0:T(8,128)(2,1)}), bf16[32,32,1,256]{3,1,2,0:T(8,128)(2,1)S(1)}, u32[]{:S(2)}, u32[]{:S(2)}) async-start(bf16[32,32,1,256]{3,1,2,0:T(8,128)(2,1)} %stack.2), calls=%async_computation | async-start | bytes 1048576 | tf_op jit(solution)/shard_map/all_to_all | solution.py:50
  74.9 8.1 %copy-start.3 = (f32[4,1024]{1,0:T(4,128)S(1)}, f32[4,1024]{1,0:T(4,128)}, u32[]{:S(2)}) copy-start(f32[4,1024]{1,0:T(4,128)} %param.16) | copy-start | bytes 49156
  74.9 55.2 %all-to-all-start.2 = ((bf16[128,12,768]{2,1,0:T(8,128)(2,1)}), bf16[128,12,768]{2,1,0:T(8,128)(2,1)}, u32[]{:S(2)}, u32[]{:S(2)}) async-start(bf16[128,12,768]{2,1,0:T(8,128)(2,1)} %broadcast_select_fusion), calls=%async_computation.2 | async-start | bytes 6291456 | tf_op jit(solution)/shard_map/all_to_all | solution.py:72
  141.5 6.3 %slice-start = ((s8[8388608]{0:T(1024)(128)(4,1)}), s8[4194304]{0:T(1024)(128)(4,1)S(1)}, s32[]{:S(2)}) async-start(s8[8388608]{0:T(1024)(128)(4,1)} %bitcast.130), calls=%async_computation.3 | async-start | bytes 8388608
  144.6 3.3 %slice-start.1 = ((s8[8388608]{0:T(1024)(128)(4,1)}), s8[4194304]{0:T(1024)(128)(4,1)S(1)}, s32[]{:S(2)}) async-start(s8[8388608]{0:T(1024)(128)(4,1)} %bitcast.130), calls=%async_computation.4 | async-start | bytes 8388608
  147.9 1.4 copy-start.5
